TPU v7x, 256 devices: a whole 4x4x8 slice. The times are simulated.
256 devices in a mesh: row: 8 (over y, core), col: 32 (over x, z).
Axes of the slice: x: 4, y: 4, z: 8, core: 2. Of those that a mesh axis runs over, the one named last changes fastest.
Arguments:
- stars: float32 [13, 524288], P(None, ('row', 'col')), may hold values from -5 to 5, as said below
- elapsed: float32 [524288], P(('row', 'col')), may hold values from 0.0625 to 0.5
- active_ids: int32 [4096], P('row'), may hold values from 0 to 524287, as said below
Outputs:
- updated_stars: float32 [13, 524288], P(None, ('row', 'col'))
Inputs may be any that keep to these rules, and one draw needn't show every extreme that they name: Rows 0 to 11 of stars hold positions, velocities, accelerations and jerks; row 12 holds masses between 0.2 / 524288 and 2 / 524288. `active_ids`: the indices are distinct.
All inputs are finite; a program needn't handle non-finite values.
Results may differ from a plain program's by a relative error of at most 0.0001.
Values sent between devices are 32-bit elements; how exact they have to be, the bound alone decides.
A program may use at most 64 MiB of HBM per device.

v0:
```python
import math

import jax
import jax.numpy as jnp
from jax import lax
from jax.sharding import PartitionSpec as P

SOFTEN = 0.0025


def predict(position, velocity, accel_old, jerk_old, elapsed):
    pos_pred = position + elapsed * (
        velocity + elapsed * (accel_old / 2.0 + elapsed * jerk_old / 6.0)
    )
    vel_pred = velocity + elapsed * (accel_old + elapsed * jerk_old / 2.0)
    return (pos_pred, vel_pred)


def pair_terms(act_pos, act_vel, fld_pos, fld_vel, fld_mass):
    offset = fld_pos[:, None, :] - act_pos[:, :, None]
    relvel = fld_vel[:, None, :] - act_vel[:, :, None]
    dist_sq = jnp.sum(offset * offset, 0) + SOFTEN
    inverse = lax.rsqrt(dist_sq)
    weight = fld_mass[None, :] * inverse * inverse * inverse
    radial = 3.0 * jnp.sum(offset * relvel, 0) * inverse * inverse
    accels = jnp.sum(weight[None] * offset, -1)
    jerk_sum = jnp.sum(weight[None] * (relvel - radial[None] * offset), -1)
    return jnp.concatenate([accels, jerk_sum], 0)


def corrector(pos_old, vel_old, acc_old, jerk_old, step_len, acc_new, jerk_new):
    vel_new = (
        vel_old
        + (acc_old + acc_new) * step_len / 2.0
        + (jerk_old - jerk_new) * step_len * step_len / 12.0
    )
    pos_new = (
        pos_old
        + (vel_old + vel_new) * step_len / 2.0
        + (acc_old - acc_new) * step_len * step_len / 12.0
    )
    return jnp.concatenate([pos_new, vel_new, acc_new, jerk_new], 0)


def local(stars, elapsed, active_ids):
    star_dev = stars.shape[1]
    act_dev = active_ids.shape[0]
    col_count = lax.axis_size("col")
    first_star = (lax.axis_index("row") * col_count + lax.axis_index("col")) * star_dev
    pos_pred, vel_pred = predict(stars[0:3], stars[3:6], stars[6:9], stars[9:12], elapsed[None, :])
    own_pred = jnp.concatenate([pos_pred, vel_pred, stars[12:13]], 0)
    field_stars = lax.all_gather(own_pred, "row", axis=1, tiled=True)
    all_idx = lax.all_gather(active_ids, "row", axis=0, tiled=True)
    local_idx = all_idx - first_star
    owned = (local_idx >= 0) & (local_idx < star_dev)
    clamped = jnp.where(owned, local_idx, 0)
    own_rows = jnp.concatenate([stars[0:12], elapsed[None, :]], 0)
    picked = jnp.where(owned[None, :], jnp.take(own_rows, clamped, axis=1), 0.0)
    summed = lax.psum(picked, ("row", "col"))
    fetched = lax.dynamic_slice_in_dim(summed, lax.axis_index("row") * act_dev, act_dev, 1)
    act_pos, act_vel = predict(
        fetched[0:3], fetched[3:6], fetched[6:9], fetched[9:12], fetched[12:13]
    )
    field_len = field_stars.shape[1]
    block_len = math.gcd(field_len, 2048)

    def add_block(block_num, running):
        field_block = lax.dynamic_slice_in_dim(field_stars, block_num * block_len, block_len, 1)
        return running + pair_terms(
            act_pos, act_vel, field_block[0:3], field_block[3:6], field_block[6]
        )

    partial_sum = lax.fori_loop(
        0, field_len // block_len, add_block, jnp.zeros((6, act_dev), jnp.float32)
    )
    totals = lax.psum(partial_sum, "col")
    target = jnp.where(owned, local_idx, star_dev)
    corrected = corrector(
        fetched[0:3],
        fetched[3:6],
        fetched[6:9],
        fetched[9:12],
        fetched[12:13],
        totals[0:3],
        totals[3:6],
    )
    gathered = lax.all_gather(corrected, "row", axis=1, tiled=True)
    updated = stars[0:12].at[:, target].set(gathered, mode="drop")
    return jnp.concatenate([updated, stars[12:13]], 0)


def solution(mesh):
    in_specs = (P(None, ("row", "col")), P(("row", "col")), P("row"))
    out_specs = P(None, ("row", "col"))
    return jax.shard_map(local, mesh=mesh, in_specs=in_specs, out_specs=out_specs, check_vma=False)
```

profile of v0, /device:TPU:1, one launch (start us, length us, event | category | flops | bytes accessed | tf_op | source)
XLA Modules:
  0.0 602.7 jit_solution(16024470177381671852)
XLA Ops:
  6.5 14.4 %all-gather = s32[8,1,512]{2,1,0:T(1,128)S(1)} all-gather(s32[1,1,512]{2,1,0:T(1,128)} %bitcast.22), channel_id=1, replica_groups=mesh['row'=8,'col'=32] {'row'}, dimensions={0}, use_global_device_ids=true | all-gather | bytes 18432 | tf_op jit(solution)/shard_map/all_gather | solution.py:53
  23.7 14.1 %gather_fusion = f32[4096,13]{1,0:T(8,128)} fusion(f32[13,2048]{0,1:T(8,128)S(1)} %pad_maximum_fusion, s32[4096]{0:T(1024)S(1)} %get-tuple-element.144), kind=kCustom, calls=%fused_computation | custom fusion | bytes 442368 | tf_op jit(solution)/shard_map/jit(_take)/gather | solution.py:58
  40.9 13.2 %all_gather.10 = f32[7,16384]{1,0:T(8,128)S(1)} all-gather(f32[7,2048]{1,0:T(8,128)S(1)} %pad_maximum_fusion.2), channel_id=1, replica_groups=mesh['row'=8,'col'=32] {'row'}, dimensions={1}, use_global_device_ids=true | all-gather | bytes 516096 | tf_op jit(solution)/shard_map/all_gather | solution.py:52
  54.0 236.2 %all-reduce.2.cloned.1.call-done = f32[13,4096]{1,0:T(8,128)} async-done(((f32[13,4096]{1,0:T(8,128)}), f32[13,4096]{1,0:T(8,128)}) %all-reduce.2.cloned.1.call-update) | async-done | bytes 213008 | tf_op jit(solution)/shard_map/psum | solution.py:59
  291.9 135.2 %while.14 = (s32[]{:T(128)}, f32[6,512]{1,0:T(8,128)S(1)}, f32[7,16384]{1,0:T(8,128)S(1)}, f32[3,512]{1,0:T(4,128)S(1)}, f32[3,512]{1,0:T(4,128)S(1)}, /*index=5...) while((s32[]{:T(128)}, f32[6,512]{1,0:T(8,128)S(1)}, ...), condition=%wide.region_6.7_spmd.clone, body=%wide.region_1.0_spmd.clone.sunk | while | flops 49289224 | bytes 33849544 | solution.py:73
  292.1 7.0 %fusion.16 = (f32[512,2048]{1,0:T(8,128)}, f32[512,2048]{1,0:T(8,128)}) fusion(f32[3,512]{1,0:T(4,128)S(1)} %get-tuple-element.218, f32[3,2048]{1,0:T(4,128)S(1)} %get-tuple-element.185, f32[3,512]{1,0:T(4,128)S(1)} %get-tuple-element.219, f32[3,2048]{1,0:T(4,128)S(1)} %get-tuple-element.186), kind=kLoop, calls=%fused_computation.9.clone.1 | loop fusion | flops 16777216 | bytes 8450048 | tf_op jit(solution)/shard_map/while/body/eval_jaxpr/reduce_sum | solution.py:22
  299.1 4.9 multiply_multiply_fusion.3
  304.0 4.8 fusion.17
  309.0 7.0 %fusion.16 = (f32[512,2048]{1,0:T(8,128)}, f32[512,2048]{1,0:T(8,128)}) fusion(f32[3,512]{1,0:T(4,128)S(1)} %get-tuple-element.218, f32[3,2048]{1,0:T(4,128)S(1)} %get-tuple-element.185, f32[3,512]{1,0:T(4,128)S(1)} %get-tuple-element.219, f32[3,2048]{1,0:T(4,128)S(1)} %get-tuple-element.186), kind=kLoop, calls=%fused_computation.9.clone.1 | loop fusion | flops 16777216 | bytes 8450048 | tf_op jit(solution)/shard_map/while/body/eval_jaxpr/reduce_sum | solution.py:22
  316.0 4.9 multiply_multiply_fusion.3
  320.9 4.8 fusion.17
  325.9 7.0 %fusion.16 = (f32[512,2048]{1,0:T(8,128)}, f32[512,2048]{1,0:T(8,128)}) fusion(f32[3,512]{1,0:T(4,128)S(1)} %get-tuple-element.218, f32[3,2048]{1,0:T(4,128)S(1)} %get-tuple-element.185, f32[3,512]{1,0:T(4,128)S(1)} %get-tuple-element.219, f32[3,2048]{1,0:T(4,128)S(1)} %get-tuple-element.186), kind=kLoop, calls=%fused_computation.9.clone.1 | loop fusion | flops 16777216 | bytes 8450048 | tf_op jit(solution)/shard_map/while/body/eval_jaxpr/reduce_sum | solution.py:22
  332.9 4.9 multiply_multiply_fusion.3
  337.8 4.8 fusion.17
  342.8 7.0 %fusion.16 = (f32[512,2048]{1,0:T(8,128)}, f32[512,2048]{1,0:T(8,128)}) fusion(f32[3,512]{1,0:T(4,128)S(1)} %get-tuple-element.218, f32[3,2048]{1,0:T(4,128)S(1)} %get-tuple-element.185, f32[3,512]{1,0:T(4,128)S(1)} %get-tuple-element.219, f32[3,2048]{1,0:T(4,128)S(1)} %get-tuple-element.186), kind=kLoop, calls=%fused_computation.9.clone.1 | loop fusion | flops 16777216 | bytes 8450048 | tf_op jit(solution)/shard_map/while/body/eval_jaxpr/reduce_sum | solution.py:22
  349.8 4.9 multiply_multiply_fusion.3
  354.7 4.8 fusion.17
  359.7 7.0 %fusion.16 = (f32[512,2048]{1,0:T(8,128)}, f32[512,2048]{1,0:T(8,128)}) fusion(f32[3,512]{1,0:T(4,128)S(1)} %get-tuple-element.218, f32[3,2048]{1,0:T(4,128)S(1)} %get-tuple-element.185, f32[3,512]{1,0:T(4,128)S(1)} %get-tuple-element.219, f32[3,2048]{1,0:T(4,128)S(1)} %get-tuple-element.186), kind=kLoop, calls=%fused_computation.9.clone.1 | loop fusion | flops 16777216 | bytes 8450048 | tf_op jit(solution)/shard_map/while/body/eval_jaxpr/reduce_sum | solution.py:22
  366.8 4.9 multiply_multiply_fusion.3
  371.6 4.8 fusion.17
  376.6 7.0 %fusion.16 = (f32[512,2048]{1,0:T(8,128)}, f32[512,2048]{1,0:T(8,128)}) fusion(f32[3,512]{1,0:T(4,128)S(1)} %get-tuple-element.218, f32[3,2048]{1,0:T(4,128)S(1)} %get-tuple-element.185, f32[3,512]{1,0:T(4,128)S(1)} %get-tuple-element.219, f32[3,2048]{1,0:T(4,128)S(1)} %get-tuple-element.186), kind=kLoop, calls=%fused_computation.9.clone.1 | loop fusion | flops 16777216 | bytes 8450048 | tf_op jit(solution)/shard_map/while/body/eval_jaxpr/reduce_sum | solution.py:22
  383.7 4.9 multiply_multiply_fusion.3
  388.5 4.8 fusion.17
  393.5 7.0 %fusion.16 = (f32[512,2048]{1,0:T(8,128)}, f32[512,2048]{1,0:T(8,128)}) fusion(f32[3,512]{1,0:T(4,128)S(1)} %get-tuple-element.218, f32[3,2048]{1,0:T(4,128)S(1)} %get-tuple-element.185, f32[3,512]{1,0:T(4,128)S(1)} %get-tuple-element.219, f32[3,2048]{1,0:T(4,128)S(1)} %get-tuple-element.186), kind=kLoop, calls=%fused_computation.9.clone.1 | loop fusion | flops 16777216 | bytes 8450048 | tf_op jit(solution)/shard_map/while/body/eval_jaxpr/reduce_sum | solution.py:22
  400.6 4.9 multiply_multiply_fusion.3
  405.4 4.8 fusion.17
  410.4 7.0 %fusion.16 = (f32[512,2048]{1,0:T(8,128)}, f32[512,2048]{1,0:T(8,128)}) fusion(f32[3,512]{1,0:T(4,128)S(1)} %get-tuple-element.218, f32[3,2048]{1,0:T(4,128)S(1)} %get-tuple-element.185, f32[3,512]{1,0:T(4,128)S(1)} %get-tuple-element.219, f32[3,2048]{1,0:T(4,128)S(1)} %get-tuple-element.186), kind=kLoop, calls=%fused_computation.9.clone.1 | loop fusion | flops 16777216 | bytes 8450048 | tf_op jit(solution)/shard_map/while/body/eval_jaxpr/reduce_sum | solution.py:22
  417.5 4.9 multiply_multiply_fusion.3
  422.3 4.8 fusion.17
  427.2 115.5 %psum.15 = f32[6,512]{1,0:T(8,128)S(1)} all-reduce(f32[6,512]{1,0:T(8,128)S(1)} %get-tuple-element.99), channel_id=1, replica_groups=mesh['row'=8,'col'=32] {'col'}, use_global_device_ids=true, to_apply=%region_7.8 | all-reduce | flops 3072 | bytes 24576 | tf_op jit(solution)/shard_map/psum | solution.py:76
  543.7 39.5 %all_gather.11 = f32[12,4096]{1,0:T(8,128)S(1)} all-gather(f32[12,512]{1,0:T(8,128)S(1)} %pad_maximum_fusion.3), channel_id=1, replica_groups=mesh['row'=8,'col'=32] {'row'}, dimensions={1}, use_global_device_ids=true | all-gather | bytes 221184 | tf_op jit(solution)/shard_map/all_gather | solution.py:87
  583.8 11.0 %scatter_fusion = f32[12,2048]{0,1:T(8,128)S(1)} fusion(f32[12,2048]{0,1:T(8,128)S(1)} %copy.57, s32[4096]{0:T(1024)S(1)} %get-tuple-element.145, f32[4096,12]{1,0:T(8,128)S(1)} %copy.55), kind=kCustom, calls=%fused_computation.1 | custom fusion | bytes 606208 | tf_op jit(solution)/shard_map/scatter | solution.py:88
  (49 shorter events, 11.6 us)
Async XLA Ops:
  6.5 283.7 %all-reduce.2.cloned.1.call-start = ((), (), s32[]{:S(2)}) async-start(), calls=%async_computation | async-start | bytes 524288 | tf_op jit(solution)/shard_map/psum | solution.py:59
  23.3 17.4 %copy-start = (f32[13,2048]{1,0:T(8,128)S(1)}, f32[13,2048]{1,0:T(8,128)}, u32[]{:S(2)}) copy-start(f32[13,2048]{1,0:T(8,128)} %param.5) | copy-start | bytes 319492
  23.3 17.4 %copy-start.1 = (f32[2048]{0:T(1024)S(1)}, f32[2048]{0:T(1024)}, u32[]{:S(2)}) copy-start(f32[2048]{0:T(1024)} %param.6) | copy-start | bytes 24580
Sparse Core Ops, SparseCore 0:
  40.9 249.3 all-reduce.1
where the time goes:
time: 603 us
  waiting for transfers between devices  236 us (39%)
  blocking collectives  183 us (30%)
  other arithmetic  137 us (23%)
  local copies, waits for them, and re-layouts  32.8 us (5%)
  between operations  13.5 us (2%)
    psum x1, waiting for transfers between devices, local(): summed = lax.psum(picked, ('row', 'col'))  236 us
    psum x1, blocking collectives, local(): totals = lax.psum(partial_sum, 'col')  116 us
    reduce_sum x8, other arithmetic, pair_terms(): dist_sq = jnp.sum(offset * offset, 0) + SOFTEN  56 us
    all_gather x1, blocking collectives, local(): gathered = lax.all_gather(corrected, 'row', axis=1, tiled=True)  39.5 us
    mul x8, other arithmetic, pair_terms(): radial = 3.0 * jnp.sum(offset * relvel, 0) * inverse * inverse  38.8 us
    reduce_sum x8, other arithmetic, pair_terms(): accels = jnp.sum(weight[None] * offset, -1)  38.4 us
    gather x2, local copies, waits for them, and re-layouts, local(): picked = jnp.where(owned[None, :], jnp.take(own_rows, clamped, axis=1), 0.0)  16.3 us
    all_gather x1, blocking collectives, local(): all_idx = lax.all_gather(active_ids, 'row', axis=0, tiled=True)  14.4 us
  transfers between devices with their start and end apart: 1, of which 1 were waited for; matrix products, arithmetic and copies ran while one was open for 0% of the time, Pallas kernels for 0%

commit v1 on v0

v1 whole, which is shorter than its diff:
```python
import functools

import jax
import jax.numpy as jnp
from jax import lax
from jax.experimental import pallas as pl
from jax.experimental.pallas import tpu as pltpu
from jax.sharding import PartitionSpec as P

SOFTEN = 0.0025
F32 = jnp.float32
BF16 = jnp.bfloat16
ROWS = 8
XS = 4
ZS = 8
STARS = 2048
ACT = 512
CHUNK = 256
SPLIT_PAIRS = ((0, 0), (0, 1), (1, 0), (1, 1), (0, 2), (2, 0))
VMEM = pl.BlockSpec(memory_space=pltpu.VMEM)


def split3(x):
    hi = x.astype(BF16).astype(F32)
    rest = x - hi
    mid = rest.astype(BF16).astype(F32)
    return hi, mid, rest - mid


def place():
    row = lax.axis_index("row")
    col = lax.axis_index("col")
    return row, col, col // ZS, col % ZS


def row_peer(o):
    row, col, _, _ = place()
    return (lax.rem(row + o, ROWS), col)


def x_peer(o):
    row, _, x, z = place()
    return (row, lax.rem(x + o, XS) * ZS + z)


def z_peer(o):
    row, _, x, z = place()
    return (row, x * ZS + lax.rem(z + o, ZS))


def enter():
    barrier = pltpu.get_barrier_semaphore()
    peers = (
        [row_peer(o) for o in range(1, ROWS)]
        + [x_peer(o) for o in range(1, XS)]
        + [z_peer(o) for o in range(1, ZS)]
    )
    for peer in peers:
        pl.semaphore_signal(barrier, inc=1, device_id=peer, device_id_type=pl.DeviceIdType.MESH)
    pl.semaphore_wait(barrier, len(peers))


def send(src, dst, send_sem, recv_sem, peer):
    copy = pltpu.make_async_remote_copy(
        src_ref=src,
        dst_ref=dst,
        send_sem=send_sem,
        recv_sem=recv_sem,
        device_id=peer,
        device_id_type=pl.DeviceIdType.MESH,
    )
    copy.start()
    return copy


def sum_over_col(own, x_in, mid, z_in, xs, xr, zs, zr):
    copies = [
        send(own, x_in.at[o - 1], xs.at[o - 1], xr.at[o - 1], x_peer(o)) for o in range(1, XS)
    ]
    for c in copies:
        c.wait()
    mid[...] = (own[...] + x_in[0]) + (x_in[1] + x_in[2])
    copies = [
        send(mid, z_in.at[o - 1], zs.at[o - 1], zr.at[o - 1], z_peer(o)) for o in range(1, ZS)
    ]
    for c in copies:
        c.wait()
    return ((mid[...] + z_in[0]) + (z_in[1] + z_in[2])) + (
        (z_in[3] + z_in[4]) + (z_in[5] + z_in[6])
    )


def gather_kernel(
    stars, elapsed, ids, field, act, own, x_in, mid, z_in, rs, rr, xs, xr, zs, zr
):
    row, col, _, _ = place()
    t = elapsed[...]
    enter()
    x, v, a, j = stars[0:3, :], stars[3:6, :], stars[6:9, :], stars[9:12, :]
    field[row, 0:3, :] = x + t * (v + t * (a / 2.0 + t * j / 6.0))
    field[row, 3:6, :] = v + t * (a + t * j / 2.0)
    field[row, 6:7, :] = stars[12:13, :]
    field[row, 7:8, :] = jnp.zeros((1, STARS), F32)
    copies = [
        send(field.at[row], field.at[row], rs.at[o - 1], rr.at[o - 1], row_peer(o))
        for o in range(1, ROWS)
    ]
    star = ids[...]
    owner = star // STARS
    group = star % STARS // 128
    lane = star % 128
    here = owner % 32 == col
    code = jnp.where(here, owner // 32 * 16 + group, -1)
    one_hot = jnp.where(
        lax.broadcasted_iota(jnp.int32, (128, ACT), 0) == lane, 1.0, 0.0
    ).astype(BF16)
    one_hot = jnp.concatenate([one_hot] * 3, 0)
    for c in copies:
        c.wait()

    def pick(r, total):
        block = jnp.concatenate([field[r, :, g * 128 : (g + 1) * 128] for g in range(16)], 0)
        parts = jnp.concatenate(split3(block), 1).astype(BF16)
        found = jnp.dot(parts, one_hot, preferred_element_type=F32)
        for g in range(16):
            total = total + jnp.where(code == r * 16 + g, found[g * 8 : (g + 1) * 8], 0.0)
        return total

    own[...] = lax.fori_loop(0, ROWS, pick, jnp.zeros((8, ACT), F32))
    act[...] = sum_over_col(own, x_in, mid, z_in, xs, xr, zs, zr)


def dither(lanes):
    return 1.0 + ((lanes * 40503) & 65535).astype(F32) * (1.0 / 65536.0)


def pair_kernel(field, act, out, bmat, rmat, acol, xib, accum, d0, d1, w0, w1):
    total = field[0]
    for r in range(1, ROWS):
        total = total + field[r]
    centre = jnp.sum(total, axis=1, keepdims=True) / (ROWS * STARS)
    cx, cv = centre[0:3], centre[3:6]
    xa, va = act[0:3, :] - cx, act[3:6, :] - cv
    sa = jnp.sum(xa * va, axis=0, keepdims=True)
    parts = split3(jnp.concatenate([-xa, -va, jnp.ones_like(sa), sa], 0))
    stacked = jnp.concatenate([parts[p] for p, _ in SPLIT_PAIRS] + [jnp.zeros((80, ACT), F32)], 0)
    acol[...] = jnp.transpose(stacked).astype(BF16)
    turned = jnp.transpose(jnp.concatenate([act[...], jnp.zeros((120, ACT), F32)], 0))
    for k in range(3):
        xib[k] = jnp.broadcast_to(turned[:, k : k + 1], (ACT, 128))
    lanes = lax.broadcasted_iota(jnp.int32, (1, STARS), 1)
    per_slot = STARS // CHUNK

    def operands(r, _):
        f = field[r]
        xf, vf, mass = f[0:3] - cx, f[3:6] - cv, f[6:7]
        sf = jnp.sum(xf * vf, axis=0, keepdims=True)
        b = split3(jnp.concatenate([vf, xf, sf, jnp.ones_like(sf)], 0))
        b = jnp.concatenate([b[q] for _, q in SPLIT_PAIRS] + [jnp.zeros((80, STARS), F32)], 0)
        b = b.astype(BF16)
        m = mass / dither(lanes)
        zero = jnp.zeros_like(m)
        by_w = jnp.concatenate([m * xf, m * vf, m, zero], 0)
        by_v = jnp.concatenate([zero, zero, zero, -3.0 * m * xf, zero, -3.0 * m], 0)
        pad = jnp.zeros((8, STARS), F32)
        by_w = jnp.concatenate(list(split3(by_w)) + [pad], 0).astype(BF16)
        by_v = jnp.concatenate(list(split3(by_v)) + [pad], 0).astype(BF16)
        for c in range(per_slot):
            cut = slice(c * CHUNK, (c + 1) * CHUNK)
            bmat[r * per_slot + c] = b[:, cut]
            rmat[r * per_slot + c] = jnp.concatenate([by_w[:, cut], by_v[:, cut]], 1)
        return 0

    lax.fori_loop(0, ROWS, operands, 0)
    accum[...] = jnp.zeros_like(accum)
    w1[...] = jnp.zeros_like(w1)
    lane = lax.broadcasted_iota(jnp.int32, (1, CHUNK), 1)
    chunks = ROWS * per_slot

    def radial(c, dst):
        dst[...] = jnp.dot(acol[...], bmat[c], preferred_element_type=F32)

    def sums(c, src):
        accum[...] += lax.dot_general(
            src[...], rmat[c], (((1,), (1,)), ((), ())), preferred_element_type=F32
        )

    def step(c, d_next, d_now, w_now, w_before):
        r = c // per_slot
        off = pl.multiple_of(c % per_slot * CHUNK, CHUNK)
        factor = dither(lane + off)
        xs = [field[r, pl.ds(k, 1), pl.ds(off, CHUNK)] for k in range(3)]
        radial(jnp.minimum(c + 1, chunks - 1), d_next)
        for h in range(CHUNK // 128):
            cut = slice(h * 128, (h + 1) * 128)
            dx, dy, dz = [xs[k][:, cut] - xib[k] for k in range(3)]
            q = (dx * dx + SOFTEN) + dy * dy + dz * dz
            inv = lax.rsqrt(q)
            inv2 = inv * inv
            w = (inv * factor[:, cut]) * inv2
            w_now[:, cut] = w.astype(BF16)
            w_now[:, CHUNK + h * 128 : CHUNK + (h + 1) * 128] = (
                w * (inv2 * d_now[:, cut])
            ).astype(BF16)
        sums(jnp.maximum(c - 1, 0), w_before)

    radial(0, d0)

    def two(i, _):
        step(2 * i, d1, d0, w0, w1)
        step(2 * i + 1, d0, d1, w1, w0)
        return 0

    lax.fori_loop(0, chunks // 2, two, 0)
    sums(chunks - 1, w1)
    o = jnp.transpose(jnp.concatenate([accum[...], jnp.zeros((ACT, 96), F32)], 1))
    o = o[0:8] + o[8:16] + o[16:24]
    out[0:3, :] = o[0:3] - xa * o[6:7]
    out[3:6, :] = o[3:6] - va * o[6:7] - xa * o[7:8]
    out[6:8, :] = jnp.zeros((2, ACT), F32)


def finish_kernel(
    part, ids, stars, elapsed, out, tot, x_in, mid, z_in, rs, rr, xs, xr, zs, zr
):
    row, col, _, _ = place()
    enter()
    total = sum_over_col(part, x_in, mid, z_in, xs, xr, zs, zr)
    tot[row, 0:6, :] = total[0:6]
    tot[row, 6:7, :] = ids[...].astype(F32)
    tot[row, 7:8, :] = jnp.ones((1, ACT), F32)
    copies = [
        send(tot.at[row], tot.at[row], rs.at[o - 1], rr.at[o - 1], row_peer(o))
        for o in range(1, ROWS)
    ]
    for c in copies:
        c.wait()
    first = (row * 32 + col) * STARS
    sub = lax.broadcasted_iota(jnp.int32, (128, ACT), 0)

    def scatter(r, sums):
        local = tot[r, 6:7, :].astype(jnp.int32) - first
        owned = (local >= 0) & (local < STARS)
        group = jnp.where(owned, local // 128, -1)
        one_hot = jnp.where(sub == local % 128, 1.0, 0.0).astype(BF16)
        parts = jnp.concatenate(split3(tot[r]), 0)
        lhs = jnp.concatenate(
            [jnp.where(group == g, parts, 0.0).astype(BF16) for g in range(16)], 0
        )
        return sums + lax.dot_general(
            lhs, one_hot, (((1,), (1,)), ((), ())), preferred_element_type=F32
        )

    placed = lax.fori_loop(0, ROWS, scatter, jnp.zeros((384, 128), F32))
    new = jnp.concatenate(
        [
            placed[g * 24 : g * 24 + 8]
            + placed[g * 24 + 8 : g * 24 + 16]
            + placed[g * 24 + 16 : g * 24 + 24]
            for g in range(16)
        ],
        1,
    )
    acc_new, jerk_new, hit = new[0:3], new[3:6], new[7:8] > 0.5
    t = elapsed[...]
    x, v, a, j = stars[0:3, :], stars[3:6, :], stars[6:9, :], stars[9:12, :]
    v1 = v + (a + acc_new) * t / 2.0 + (j - jerk_new) * t * t / 12.0
    x1 = x + (v + v1) * t / 2.0 + (a - acc_new) * t * t / 12.0
    out[0:3, :] = jnp.where(hit, x1, x)
    out[3:6, :] = jnp.where(hit, v1, v)
    out[6:9, :] = jnp.where(hit, acc_new, a)
    out[9:12, :] = jnp.where(hit, jerk_new, j)
    out[12:13, :] = stars[12:13, :]


def exchange_scratch():
    dma = pltpu.SemaphoreType.DMA
    return [
        pltpu.VMEM((XS - 1, 8, ACT), F32),
        pltpu.VMEM((8, ACT), F32),
        pltpu.VMEM((ZS - 1, 8, ACT), F32),
        dma((ROWS - 1,)),
        dma((ROWS - 1,)),
        dma((XS - 1,)),
        dma((XS - 1,)),
        dma((ZS - 1,)),
        dma((ZS - 1,)),
    ]


def local(stars, elapsed, active_ids):
    elapsed = elapsed.reshape(1, STARS)
    ids = active_ids.reshape(1, ACT)
    field, act = pl.pallas_call(
        gather_kernel,
        out_shape=(
            jax.ShapeDtypeStruct((ROWS, 8, STARS), F32),
            jax.ShapeDtypeStruct((8, ACT), F32),
        ),
        in_specs=[VMEM] * 3,
        out_specs=(VMEM, VMEM),
        scratch_shapes=[pltpu.VMEM((8, ACT), F32)] + exchange_scratch(),
        compiler_params=pltpu.CompilerParams(
            collective_id=0, has_side_effects=True, vmem_limit_bytes=32 << 20
        ),
        name="gather_active",
    )(stars, elapsed, ids)
    part = pl.pallas_call(
        pair_kernel,
        out_shape=jax.ShapeDtypeStruct((8, ACT), F32),
        in_specs=[VMEM] * 2,
        out_specs=VMEM,
        scratch_shapes=[
            pltpu.VMEM((64, 128, CHUNK), BF16),
            pltpu.VMEM((64, 32, 2 * CHUNK), BF16),
            pltpu.VMEM((ACT, 128), BF16),
            pltpu.VMEM((3, ACT, 128), F32),
            pltpu.VMEM((ACT, 32), F32),
            pltpu.VMEM((ACT, CHUNK), F32),
            pltpu.VMEM((ACT, CHUNK), F32),
            pltpu.VMEM((ACT, 2 * CHUNK), BF16),
            pltpu.VMEM((ACT, 2 * CHUNK), BF16),
        ],
        compiler_params=pltpu.CompilerParams(vmem_limit_bytes=40 << 20),
        name="pair_sums",
    )(field, act)
    return pl.pallas_call(
        finish_kernel,
        out_shape=jax.ShapeDtypeStruct((13, STARS), F32),
        in_specs=[VMEM] * 4,
        out_specs=VMEM,
        scratch_shapes=[pltpu.VMEM((ROWS, 8, ACT), F32)] + exchange_scratch(),
        compiler_params=pltpu.CompilerParams(
            collective_id=1, has_side_effects=True, vmem_limit_bytes=32 << 20
        ),
        name="finish_active",
    )(part, ids, stars, elapsed)


def solution(mesh):
    in_specs = (P(None, ("row", "col")), P(("row", "col")), P("row"))
    out_specs = P(None, ("row", "col"))
    return jax.shard_map(local, mesh=mesh, in_specs=in_specs, out_specs=out_specs, check_vma=False)
```

time: 603 us -> 83.1 us (0.14)
  waiting for transfers between devices: 236 us -> 0 us
  blocking collectives: 183 us -> 0 us
  other arithmetic: 137 us -> 0 us
  Pallas kernels: 0 us -> 79.9 us
  local copies, waits for them, and re-layouts: 32.8 us -> 2.95 us
  between operations: 13.5 us -> 0.04 us
    psum x1 -> x0, waiting for transfers between devices: 236 us -> none  [local(): summed = lax.psum(picked, ('row', 'col'))]
    psum x1 -> x0, blocking collectives: 116 us -> none  [local(): totals = lax.psum(partial_sum, 'col')]
    reduce_sum x16 -> x0, other arithmetic: 94.5 us -> none  [the longest x8 56 us: pair_terms(): dist_sq = jnp.sum(offset * offset, 0) + SOFTEN]
    pallas_call x0 -> x3, Pallas kernels: none -> 79.9 us  [the longest x1 31.7 us: local(): pl.pallas_call(pair_kernel, out_shape=jax.ShapeDtypeStruct((8, ACT), F32)...]
    all_gather x3 -> x0, blocking collectives: 67 us -> none  [the longest x1 39.5 us: local(): gathered = lax.all_gather(corrected, 'row', axis=1, tiled=True)]
    mul x8 -> x0, other arithmetic: 38.8 us -> none  [pair_terms(): radial = 3.0 * jnp.sum(offset * relvel, 0) * inverse * inverse]
    gather x2 -> x0, local copies, waits for them, and re-layouts: 16.3 us -> none  [local(): picked = jnp.where(owned[None, :], jnp.take(own_rows, clamped, axis=1), 0.0)]
    scatter x2 -> x0, local copies, waits for them, and re-layouts: 11.3 us -> none  [local(): updated = stars[0:12].at[:, target].set(gathered, mode='drop')]
  transfers between devices with their start and end apart: 1 -> 0, of which waited for: 1 -> 0; matrix products, arithmetic and copies ran while one was open for 0% -> 0% of each run, Pallas kernels for 0% -> 0%
where the time goes in v1:
time: 83.1 us; the launch traced here: 82.9 us
  Pallas kernels  79.9 us (96%)
  local copies, waits for them, and re-layouts  2.95 us (4%)
    pallas_call x1, Pallas kernels, local(): pl.pallas_call(pair_kernel, out_shape=jax.ShapeDtypeStruct((8, ACT), F32)...  31.7 us
    pallas_call x1, Pallas kernels, local(): pl.pallas_call(gather_kernel, out_shape=(jax.ShapeDtypeStruct((ROWS, 8, S...  27.7 us
    pallas_call x1, Pallas kernels, local(): pl.pallas_call(finish_kernel, out_shape=jax.ShapeDtypeStruct((13, STARS),...  20.5 us
    unnamed x11, local copies, waits for them, and re-layouts  2.95 us

profile of v1, /device:TPU:1, one launch (start us, length us, event | category | flops | bytes accessed | tf_op | source)
XLA Modules:
  0.0 82.9 jit_solution(8586795285093257519)
XLA Ops:
  0.0 0.0 copy-start.4
  0.0 0.7 copy-done.4
  0.7 0.0 copy-start
  0.7 0.9 %copy-done = f32[13,2048]{1,0:T(8,128)S(1)} copy-done((f32[13,2048]{1,0:T(8,128)S(1)}, f32[13,2048]{1,0:T(8,128)}, u32[]{:S(2)}) %copy-start) | copy-done | bytes 106520
  1.6 0.0 copy-start.2
  1.6 0.7 copy-done.2
  2.3 27.7 %gather_active.1 = (f32[8,8,2048]{2,1,0:T(8,128)S(1)}, f32[8,512]{1,0:T(8,128)S(1)}) custom-call(f32[13,2048]{1,0:T(8,128)S(1)} %copy-done, f32[1,2048]{1,0:T(1,128)S(1)} %bitcast.2, s32[1,512]{1,0:T(1,128)S(1)} %bitcast.4), custom_call_target="tpu_custom_call" | custom-call | tf_op jit(solution)/shard_map/gather_active/pallas_call | solution.py:294
  30.0 0.0 copy-start.1
  30.1 0.0 copy-start.3
  30.1 31.7 %pair_sums.1.part = f32[8,512]{1,0:T(8,128)S(1)} custom-call(f32[8,8,2048]{2,1,0:T(8,128)S(1)} %get-tuple-element.7.field, f32[8,512]{1,0:T(8,128)S(1)} %get-tuple-element.8.act), custom_call_target="tpu_custom_call" | custom-call | tf_op jit(solution)/shard_map/pair_sums/pallas_call | solution.py:308
  61.7 0.0 copy-done.1
  61.7 0.0 copy-done.3
  61.8 20.5 %finish_active.1 = f32[13,2048]{1,0:T(8,128)S(1)} custom-call(f32[8,512]{1,0:T(8,128)S(1)} %pair_sums.1.part, s32[1,512]{1,0:T(1,128)S(1)} %bitcast.5, f32[13,2048]{1,0:T(8,128)S(1)} %copy-done.1, f32[1,2048]{1,0:T(1,128)S(1)} %bitcast.3), custom_call_target="tpu_custom_call" | custom-call | tf_op jit(solution)/shard_map/finish_active/pallas_call | solution.py:327
  82.3 0.7 copy.5
Async XLA Ops:
  0.0 0.7 copy-start.4
  0.7 0.9 %copy-start = (f32[13,2048]{1,0:T(8,128)S(1)}, f32[13,2048]{1,0:T(8,128)}, u32[]{:S(2)}) copy-start(f32[13,2048]{1,0:T(8,128)} %stars.3) | copy-start | bytes 319492
  1.6 0.7 copy-start.2
  30.0 31.7 %copy-start.1 = (f32[13,2048]{1,0:T(8,128)S(1)}, f32[13,2048]{1,0:T(8,128)}, u32[]{:S(2)}) copy-start(f32[13,2048]{1,0:T(8,128)} %stars.3) | copy-start | bytes 319492
  30.1 31.7 %copy-start.3 = (f32[2048]{0:T(1024)S(1)}, f32[2048]{0:T(1024)}, u32[]{:S(2)}) copy-start(f32[2048]{0:T(1024)} %param.4) | copy-start | bytes 24580

commit v2 on v0

v2 whole, which is shorter than its diff:
```python
import jax
import jax.numpy as jnp
import numpy as np
from jax import lax
from jax.experimental import pallas as pl
from jax.experimental.pallas import tpu as pltpu
from jax.sharding import PartitionSpec as P

SOFTEN = 0.0025
F32 = jnp.float32
BF16 = jnp.bfloat16
ROWS = 8
YS = 4
XS = 4
ZS = 8
COLS = XS * ZS
STARS = 2048
ACT = 512
CHUNK = 256
PER_SLOT = STARS // CHUNK
CHUNKS = ROWS * PER_SLOT
UNROLL = 4
BLOCK = 64
SPAN = 256
GROUPS = STARS // SPAN
SPLIT_PAIRS = ((0, 0), (0, 1), (1, 0), (1, 1), (0, 2), (2, 0))
SOFTEN_HI = float(np.float32(SOFTEN).astype(jnp.bfloat16))
SOFTEN_LO = float(np.float32(SOFTEN - SOFTEN_HI).astype(jnp.bfloat16))
VMEM = pl.BlockSpec(memory_space=pltpu.VMEM)
HBM = pl.BlockSpec(memory_space=pl.ANY)


def split3(x):
    hi = x.astype(BF16).astype(F32)
    rest = x - hi
    mid = rest.astype(BF16).astype(F32)
    return hi, mid, rest - mid


def split_grid(x):
    coarse = jnp.floor(x * 8.0 + 0.5) * 0.125
    return coarse, x - coarse


def dot3(a, b):
    return jnp.sum(a * b, axis=0, keepdims=True)


def place():
    row = lax.axis_index("row")
    col = lax.axis_index("col")
    return row, col, row // 2, row % 2, col // ZS, col % ZS


def row_from(o):
    _, _, y, core, _, _ = place()
    return lax.rem(y + YS - o, YS) * 2 + core


def y_peer(o):
    _, col, y, core, _, _ = place()
    return (lax.rem(y + o, YS) * 2 + core, col)


def sibling():
    _, col, y, core, _, _ = place()
    return (y * 2 + 1 - core, col)


def x_peer(o):
    row, _, _, _, x, z = place()
    return (row, lax.rem(x + o, XS) * ZS + z)


def z_peer(o):
    row, _, _, _, x, z = place()
    return (row, x * ZS + lax.rem(z + o, ZS))


def send(src, dst, send_sem, recv_sem, peer):
    copy = pltpu.make_async_remote_copy(
        src_ref=src,
        dst_ref=dst,
        send_sem=send_sem,
        recv_sem=recv_sem,
        device_id=peer,
        device_id_type=pl.DeviceIdType.MESH,
    )
    copy.start()
    return copy


def dither(lanes):
    return 1.0 + ((lanes * 40503) & 127).astype(F32) * (1.0 / 128.0)


def field_rows(x, v):
    coarse, fine = split_grid(x)
    one = jnp.ones_like(x[0:1])
    zero = jnp.zeros_like(one)
    big = split3(dot3(coarse, coarse))
    small = split3(dot3(2.0 * coarse + fine, fine))
    hi, mid, lo = split3(fine)
    radial = split3(jnp.concatenate([v, x, dot3(x, v), one], 0))
    return jnp.concatenate(
        [*big, one, one, one, -2.0 * coarse]
        + [zero] * 7
        + [-2.0 * coarse] * 3
        + [hi, mid, lo, -2.0 * hi, -2.0 * hi, -2.0 * mid, -2.0 * mid, *small]
        + [one] * 5
        + [zero] * 10
        + [radial[q] for _, q in SPLIT_PAIRS]
        + [zero] * 16,
        0,
    )


def active_rows(x, v):
    coarse, fine = split_grid(x)
    one = jnp.ones_like(x[0:1])
    zero = jnp.zeros_like(one)
    big = split3(dot3(coarse, coarse))
    small = split3(dot3(2.0 * coarse + fine, fine))
    hi, mid, lo = split3(fine)
    radial = split3(jnp.concatenate([-x, -v, one, dot3(x, v)], 0))
    for_q = jnp.concatenate(
        [one, one, one, *big, coarse]
        + [zero] * 7
        + [hi, mid, lo]
        + [-2.0 * coarse] * 3
        + [hi, mid, hi, mid, one, one, one, *small, SOFTEN_HI * one, SOFTEN_LO * one]
        + [zero] * 74,
        0,
    )
    for_d = jnp.concatenate(
        [zero] * 64 + [radial[p] for p, _ in SPLIT_PAIRS] + [zero] * 16, 0
    )
    return jnp.concatenate([for_q, for_d], 1).astype(BF16)


def kernel(
    stars_in,
    elapsed_in,
    ids_in,
    out,
    stars,
    elapsed,
    ids,
    field,
    found,
    act_x,
    act_mid,
    act_z,
    feats,
    mix,
    spots,
    act_w,
    factor,
    accum,
    qd0,
    qd1,
    w0,
    w1,
    part,
    sum_x,
    sum_mid,
    sum_z,
    tot,
    in_sem,
    fy_s,
    fy_r,
    fc_s,
    fc_r,
    ax_s,
    ax_r,
    az_s,
    az_r,
    sx_s,
    sx_r,
    sz_s,
    sz_r,
    ty_s,
    ty_r,
    tc_s,
    tc_r,
):
    row, col, _, core, _, _ = place()
    loads = [
        pltpu.make_async_copy(src, dst, in_sem.at[i])
        for i, (src, dst) in enumerate(((stars_in, stars), (elapsed_in, elapsed), (ids_in, ids)))
    ]
    for c in loads:
        c.start()
    barrier = pltpu.get_barrier_semaphore()
    peers = (
        [sibling()]
        + [y_peer(o) for o in range(1, YS)]
        + [x_peer(o) for o in range(1, XS)]
        + [z_peer(o) for o in range(1, ZS)]
    )
    for peer in peers:
        pl.semaphore_signal(barrier, inc=1, device_id=peer, device_id_type=pl.DeviceIdType.MESH)
    for c in loads:
        c.wait()

    t = elapsed[...]
    x, v, a, j = stars[0:3, :], stars[3:6, :], stars[6:9, :], stars[9:12, :]
    x = x + t * (v + t * (a / 2.0 + t * j / 6.0))
    v = v + t * (a + t * j / 2.0)
    field[row, 0:3, :] = x
    field[row, 3:6, :] = v
    field[row, 6:7, :] = stars[12:13, :]
    star = ids[...]
    field[row, 7:8, :] = jnp.concatenate([star.astype(F32), jnp.zeros((1, STARS - ACT), F32)], 1)
    centre_x = jnp.floor(jnp.sum(x, axis=1, keepdims=True) * (8.0 / STARS) + 0.5) * 0.125
    centre_v = jnp.floor(jnp.sum(v, axis=1, keepdims=True) * (8.0 / STARS) + 0.5) * 0.125
    pl.semaphore_wait(barrier, len(peers))

    waits = []
    own = field.at[row]
    over_y = {o: send(own, own, fy_s.at[o - 1], fy_r.at[o - 1], y_peer(o)) for o in (1, 3, 2)}
    over_core = [send(own, own, fc_s.at[0], fc_r.at[0], sibling())]

    owner = star // STARS
    code = jnp.where(owner % COLS == col, owner // COLS * 16 + star % STARS // 128, -1)
    one_hot = jnp.where(
        lax.broadcasted_iota(jnp.int32, (128, ACT), 0) == star % 128, 1.0, 0.0
    ).astype(BF16)
    one_hot = jnp.concatenate([one_hot] * 3, 0)

    def pick(r):
        block = jnp.concatenate([field[r, :, g * 128 : (g + 1) * 128] for g in range(16)], 0)
        parts = jnp.concatenate(split3(block), 1).astype(BF16)
        hits = jnp.dot(parts, one_hot, preferred_element_type=F32)
        total = jnp.zeros((8, ACT), F32)
        for g in range(16):
            total = total + jnp.where(code == r * 16 + g, hits[g * 8 : (g + 1) * 8], 0.0)
        found[...] += total

    found[...] = jnp.zeros_like(found)
    pick(row)
    for o in (1, 3, 2):
        over_y[o].wait_recv()
        block = field.at[row_from(o)]
        over_core.append(send(block, block, fc_s.at[o], fc_r.at[o], sibling()))
        pick(row_from(o))
    for c, o in zip(over_core, (0, 1, 3, 2)):
        c.wait_recv()
        pick(row_from(o) + 1 - 2 * core)
    waits += list(over_y.values()) + over_core

    lanes = lax.broadcasted_iota(jnp.int32, (1, STARS), 1)
    lane_of = lax.broadcasted_iota(jnp.int32, (SPAN, ACT), 0)

    def operands(r, _):
        f = field[r]
        x, v, mass = f[0:3] - centre_x, f[3:6] - centre_v, f[6:7]
        rows = field_rows(x, v)
        for b in range(STARS // 128):
            at = pl.ds(pl.multiple_of(r * STARS + b * 128, 128), 128)
            feats[at, :] = jnp.transpose(rows[:, b * 128 : (b + 1) * 128]).astype(BF16)
        m = mass / dither(lanes & 127)
        zero = jnp.zeros_like(m)
        by_w = jnp.concatenate([m * x, m * v, m, zero], 0)
        m = -3.0 * m
        by_v = jnp.concatenate([zero, zero, zero, m * x, zero, m], 0)
        pad = jnp.zeros((8, STARS), F32)
        by_w = jnp.concatenate([*split3(by_w), pad], 0).astype(BF16)
        by_v = jnp.concatenate([*split3(by_v), pad], 0).astype(BF16)
        for c in range(PER_SLOT):
            cut = slice(c * CHUNK, (c + 1) * CHUNK)
            mix[r * PER_SLOT + c] = jnp.concatenate([by_w[:, cut], by_v[:, cut]], 1)
        at = f[7:8, 0:ACT].astype(jnp.int32) % SPAN
        spots[r] = jnp.where(lane_of == at, 1.0, 0.0).astype(BF16)
        return 0

    copies = [
        send(found, act_x.at[o - 1], ax_s.at[o - 1], ax_r.at[o - 1], x_peer(o))
        for o in range(1, XS)
    ]
    factor[...] = dither(lax.broadcasted_iota(jnp.int32, (128, 128), 0))
    lax.fori_loop(0, 4, operands, 0)
    for c in copies:
        c.wait_recv()
    waits += copies
    act_mid[...] = (found[...] + act_x[0]) + (act_x[1] + act_x[2])
    copies = [
        send(act_mid, act_z.at[o - 1], az_s.at[o - 1], az_r.at[o - 1], z_peer(o))
        for o in range(1, ZS)
    ]
    lax.fori_loop(4, ROWS, operands, 0)
    accum[...] = jnp.zeros_like(accum)
    w1[...] = jnp.zeros_like(w1)
    for c in copies:
        c.wait_recv()
    waits += copies
    act = act_mid[...]
    for o in range(ZS - 1):
        act = act + act_z[o]
    xa, va = act[0:3] - centre_x, act[3:6] - centre_v
    act_w[...] = active_rows(xa, va)

    def sums(c, w):
        accum[...] += jnp.dot(mix[c], w[...], preferred_element_type=F32)

    def step(c, qd, w_now, w_before):
        at = pl.ds(pl.multiple_of(c * CHUNK, CHUNK), CHUNK)
        qd[...] = jnp.dot(feats[at, :], act_w[...], preferred_element_type=F32)
        sums(jnp.maximum(c - 1, 0), w_before)
        for b in range(CHUNK // BLOCK):
            down = slice(b * BLOCK, (b + 1) * BLOCK)
            below = slice(CHUNK + b * BLOCK, CHUNK + (b + 1) * BLOCK)
            f = factor[b * BLOCK % 128 : b * BLOCK % 128 + BLOCK, :]
            for h in range(ACT // 128):
                cut = slice(h * 128, (h + 1) * 128)
                inv = lax.rsqrt(qd[down, cut])
                inv2 = inv * inv
                w = (inv * f) * inv2
                w_now[down, cut] = w.astype(BF16)
                d = qd[down, ACT + h * 128 : ACT + (h + 1) * 128]
                w_now[below, cut] = (w * (inv2 * d)).astype(BF16)

    def steps(i, _):
        for u in range(0, UNROLL, 2):
            step(UNROLL * i + u, qd0, w0, w1)
            step(UNROLL * i + u + 1, qd1, w1, w0)
        return 0

    lax.fori_loop(0, CHUNKS // UNROLL, steps, 0)
    sums(CHUNKS - 1, w1)
    o = accum[...]
    o = o[0:8] + o[8:16] + o[16:24]
    part[0:3, :] = o[0:3] - xa * o[6:7]
    part[3:6, :] = o[3:6] - va * o[6:7] - xa * o[7:8]
    part[6:8, :] = jnp.zeros((2, ACT), F32)

    copies = [
        send(part, sum_x.at[o - 1], sx_s.at[o - 1], sx_r.at[o - 1], x_peer(o))
        for o in range(1, XS)
    ]
    for c in copies:
        c.wait_recv()
    waits += copies
    sum_mid[...] = (part[...] + sum_x[0]) + (sum_x[1] + sum_x[2])
    copies = [
        send(sum_mid, sum_z.at[o - 1], sz_s.at[o - 1], sz_r.at[o - 1], z_peer(o))
        for o in range(1, ZS)
    ]
    for c in copies:
        c.wait_recv()
    waits += copies
    total = ((sum_mid[...] + sum_z[0]) + (sum_z[1] + sum_z[2])) + (
        (sum_z[3] + sum_z[4]) + (sum_z[5] + sum_z[6])
    )
    tot[row, 0:6, :] = total[0:6]
    tot[row, 6:7, :] = jnp.zeros((1, ACT), F32)
    tot[row, 7:8, :] = jnp.ones((1, ACT), F32)
    own = tot.at[row]
    over_y = {o: send(own, own, ty_s.at[o - 1], ty_r.at[o - 1], y_peer(o)) for o in (1, 3, 2)}
    over_core = [send(own, own, tc_s.at[0], tc_r.at[0], sibling())]

    first = (row * COLS + col) * STARS

    def scatter(r):
        local = field[r, 7:8, 0:ACT].astype(jnp.int32) - first
        group = jnp.where((local >= 0) & (local < STARS), local // SPAN, -1)
        parts = jnp.concatenate(split3(tot[r]), 0)
        lhs = jnp.concatenate([jnp.where(group == g, parts, 0.0) for g in range(GROUPS)], 0)
        return lax.dot_general(
            lhs.astype(BF16), spots[r], (((1,), (1,)), ((), ())), preferred_element_type=F32
        )

    placed = scatter(row)
    for o in (1, 3, 2):
        over_y[o].wait_recv()
        block = tot.at[row_from(o)]
        over_core.append(send(block, block, tc_s.at[o], tc_r.at[o], sibling()))
        placed = placed + scatter(row_from(o))
    for c, o in zip(over_core, (0, 1, 3, 2)):
        c.wait_recv()
        placed = placed + scatter(row_from(o) + 1 - 2 * core)
    waits += list(over_y.values()) + over_core
    new = jnp.concatenate(
        [
            placed[g * 24 : g * 24 + 8]
            + placed[g * 24 + 8 : g * 24 + 16]
            + placed[g * 24 + 16 : g * 24 + 24]
            for g in range(GROUPS)
        ],
        1,
    )
    acc_new, jerk_new, hit = new[0:3], new[3:6], new[7:8] > 0.5
    t = elapsed[...]
    x, v, a, j = stars[0:3, :], stars[3:6, :], stars[6:9, :], stars[9:12, :]
    v1 = v + (a + acc_new) * t / 2.0 + (j - jerk_new) * t * t / 12.0
    x1 = x + (v + v1) * t / 2.0 + (a - acc_new) * t * t / 12.0
    out[0:3, :] = jnp.where(hit, x1, x)
    out[3:6, :] = jnp.where(hit, v1, v)
    out[6:9, :] = jnp.where(hit, acc_new, a)
    out[9:12, :] = jnp.where(hit, jerk_new, j)
    out[12:13, :] = stars[12:13, :]
    for c in waits:
        c.wait_send()


def scratch():
    dma = pltpu.SemaphoreType.DMA

    def sums():
        return [
            pltpu.VMEM((8, ACT), F32),
            pltpu.VMEM((XS - 1, 8, ACT), F32),
            pltpu.VMEM((8, ACT), F32),
            pltpu.VMEM((ZS - 1, 8, ACT), F32),
        ]

    return (
        [
            pltpu.VMEM((13, STARS), F32),
            pltpu.VMEM((1, STARS), F32),
            pltpu.VMEM((1, ACT), jnp.int32),
            pltpu.VMEM((ROWS, 8, STARS), F32),
        ]
        + sums()
        + [
            pltpu.VMEM((ROWS * STARS, 128), BF16),
            pltpu.VMEM((CHUNKS, 32, 2 * CHUNK), BF16),
            pltpu.VMEM((ROWS, SPAN, ACT), BF16),
            pltpu.VMEM((128, 2 * ACT), BF16),
            pltpu.VMEM((128, 128), F32),
            pltpu.VMEM((32, ACT), F32),
            pltpu.VMEM((CHUNK, 2 * ACT), F32),
            pltpu.VMEM((CHUNK, 2 * ACT), F32),
            pltpu.VMEM((2 * CHUNK, ACT), BF16),
            pltpu.VMEM((2 * CHUNK, ACT), BF16),
        ]
        + sums()
        + [pltpu.VMEM((ROWS, 8, ACT), F32), dma((3,))]
        + [dma((n,)) for n in (YS - 1, YS - 1, YS, YS)]
        + [dma((n,)) for n in (XS - 1, XS - 1, ZS - 1, ZS - 1) * 2]
        + [dma((n,)) for n in (YS - 1, YS - 1, YS, YS)]
    )


def local(stars, elapsed, active_ids):
    return pl.pallas_call(
        kernel,
        out_shape=pltpu.VMEM((13, STARS), F32),
        in_specs=[HBM] * 3,
        out_specs=VMEM,
        scratch_shapes=scratch(),
        compiler_params=pltpu.CompilerParams(
            collective_id=0, has_side_effects=True, vmem_limit_bytes=56 << 20
        ),
        name="hermite_step",
    )(stars, elapsed.reshape(1, STARS), active_ids.reshape(1, ACT))


def solution(mesh):
    in_specs = (P(None, ("row", "col")), P(("row", "col")), P("row"))
    out_specs = P(None, ("row", "col"))
    return jax.shard_map(local, mesh=mesh, in_specs=in_specs, out_specs=out_specs, check_vma=False)
```

time: 603 us -> 59.3 us (0.10)
  waiting for transfers between devices: 236 us -> 0 us
  blocking collectives: 183 us -> 0 us
  other arithmetic: 137 us -> 0 us
  Pallas kernels: 0 us -> 58.5 us
  local copies, waits for them, and re-layouts: 32.8 us -> 0.66 us
  between operations: 13.5 us -> 0.01 us
    psum x1 -> x0, waiting for transfers between devices: 236 us -> none  [local(): summed = lax.psum(picked, ('row', 'col'))]
    psum x1 -> x0, blocking collectives: 116 us -> none  [local(): totals = lax.psum(partial_sum, 'col')]
    reduce_sum x16 -> x0, other arithmetic: 94.5 us -> none  [the longest x8 56 us: pair_terms(): dist_sq = jnp.sum(offset * offset, 0) + SOFTEN]
    all_gather x3 -> x0, blocking collectives: 67 us -> none  [the longest x1 39.5 us: local(): gathered = lax.all_gather(corrected, 'row', axis=1, tiled=True)]
    pallas_call x0 -> x1, Pallas kernels: none -> 58.5 us  [local(): pl.pallas_call(kernel, out_shape=pltpu.VMEM((13, STARS), F32), in_specs=[...]
    mul x8 -> x0, other arithmetic: 38.8 us -> none  [pair_terms(): radial = 3.0 * jnp.sum(offset * relvel, 0) * inverse * inverse]
    gather x2 -> x0, local copies, waits for them, and re-layouts: 16.3 us -> none  [local(): picked = jnp.where(owned[None, :], jnp.take(own_rows, clamped, axis=1), 0.0)]
    scatter x2 -> x0, local copies, waits for them, and re-layouts: 11.3 us -> none  [local(): updated = stars[0:12].at[:, target].set(gathered, mode='drop')]
  transfers between devices with their start and end apart: 1 -> 0, of which waited for: 1 -> 0; matrix products, arithmetic and copies ran while one was open for 0% -> 0% of each run, Pallas kernels for 0% -> 0%
where the time goes in v2:
time: 59.3 us; the launch traced here: 59.2 us
  Pallas kernels  58.5 us (99%)
  local copies, waits for them, and re-layouts  0.66 us (1%)
    pallas_call x1, Pallas kernels, local(): pl.pallas_call(kernel, out_shape=pltpu.VMEM((13, STARS), F32), in_specs=[...  58.5 us

profile of v2, /device:TPU:1, one launch (start us, length us, event | category | flops | bytes accessed | tf_op | source)
XLA Modules:
  0.0 59.2 jit_solution(1136817626254624354)
XLA Ops:
  0.0 58.5 %hermite_step.1 = f32[13,2048]{1,0:T(8,128)S(1)} custom-call(f32[13,2048]{1,0:T(8,128)} %stars_in.1, f32[1,2048]{1,0:T(1,128)} %bitcast.2, s32[1,512]{1,0:T(1,128)} %bitcast.3), custom_call_target="tpu_custom_call" | custom-call | tf_op jit(solution)/shard_map/hermite_step/pallas_call | solution.py:446
  58.5 0.7 %copy.5 = f32[13,2048]{1,0:T(8,128)} copy(f32[13,2048]{1,0:T(8,128)S(1)} %hermite_step.1) | data formatting | bytes 212992

commit v3 on v2

--- a/solution.py
+++ b/solution.py
@@ -19,7 +19,8 @@
 CHUNK = 256
 PER_SLOT = STARS // CHUNK
 CHUNKS = ROWS * PER_SLOT
-UNROLL = 4
+UNROLL = 16
+HALF = 256
 BLOCK = 64
 SPAN = 256
 GROUPS = STARS // SPAN
@@ -300,13 +301,21 @@
     xa, va = act[0:3] - centre_x, act[3:6] - centre_v
     act_w[...] = active_rows(xa, va)
 
-    def sums(c, w):
-        accum[...] += jnp.dot(mix[c], w[...], preferred_element_type=F32)
+    def products(c, qd, h, z):
+        at = pl.ds(pl.multiple_of(c * CHUNK, CHUNK), CHUNK)
+        cut = slice(z * ACT + h * HALF, z * ACT + (h + 1) * HALF)
+        qd[:, cut] = jnp.dot(feats[at, :], act_w[:, cut], preferred_element_type=F32)
+
+    def sums(c, w, h):
+        cut = slice(h * HALF, (h + 1) * HALF)
+        accum[:, cut] += jnp.dot(mix[c], w[:, cut], preferred_element_type=F32)
 
     def step(c, qd, w_now, w_before):
-        at = pl.ds(pl.multiple_of(c * CHUNK, CHUNK), CHUNK)
-        qd[...] = jnp.dot(feats[at, :], act_w[...], preferred_element_type=F32)
-        sums(jnp.maximum(c - 1, 0), w_before)
+        before = jnp.maximum(c - 1, 0)
+        for h in range(ACT // HALF):
+            products(c, qd, h, 0)
+            products(c, qd, h, 1)
+            sums(before, w_before, h)
         for b in range(CHUNK // BLOCK):
             down = slice(b * BLOCK, (b + 1) * BLOCK)
             below = slice(CHUNK + b * BLOCK, CHUNK + (b + 1) * BLOCK)
@@ -327,7 +336,8 @@
         return 0
 
     lax.fori_loop(0, CHUNKS // UNROLL, steps, 0)
-    sums(CHUNKS - 1, w1)
+    for h in range(ACT // HALF):
+        sums(CHUNKS - 1, w1, h)
     o = accum[...]
     o = o[0:8] + o[8:16] + o[16:24]
     part[0:3, :] = o[0:3] - xa * o[6:7]

time: 59.3 us -> 55.1 us (0.929)
  Pallas kernels: 58.5 us -> 54.4 us
    pallas_call x1, Pallas kernels: 58.5 us -> 54.4 us  [local(): pl.pallas_call(kernel, out_shape=pltpu.VMEM((13, STARS), F32), in_specs=[...]
where the time goes in v3:
time: 55.1 us; the launch traced here: 55 us
  Pallas kernels  54.4 us (99%)
  local copies, waits for them, and re-layouts  0.66 us (1%)
    pallas_call x1, Pallas kernels, local(): pl.pallas_call(kernel, out_shape=pltpu.VMEM((13, STARS), F32), in_specs=[...  54.4 us

profile of v3, /device:TPU:1, one launch (start us, length us, event | category | flops | bytes accessed | tf_op | source)
XLA Modules:
  0.0 55.0 jit_solution(15083327171726875170)
XLA Ops:
  0.0 54.4 %hermite_step.1 = f32[13,2048]{1,0:T(8,128)S(1)} custom-call(f32[13,2048]{1,0:T(8,128)} %stars_in.1, f32[1,2048]{1,0:T(1,128)} %bitcast.2, s32[1,512]{1,0:T(1,128)} %bitcast.3), custom_call_target="tpu_custom_call" | custom-call | tf_op jit(solution)/shard_map/hermite_step/pallas_call | solution.py:456
  54.4 0.7 %copy.5 = f32[13,2048]{1,0:T(8,128)} copy(f32[13,2048]{1,0:T(8,128)S(1)} %hermite_step.1) | data formatting | bytes 212992

commit v4 on v3

--- a/solution.py
+++ b/solution.py
@@ -22,6 +22,10 @@
 UNROLL = 16
 HALF = 256
 BLOCK = 64
+Y_ORDER = (2, 1, 3)
+X_ORDER = (2, 1, 3)
+Z_ORDER = (4, 3, 5, 2, 6, 1, 7)
+PLANE = [(oy, ox) for oy in (2, 1, 3, 0) for ox in (2, 1, 3, 0) if (oy, ox) != (0, 0)]
 SPAN = 256
 GROUPS = STARS // SPAN
 SPLIT_PAIRS = ((0, 0), (0, 1), (1, 0), (1, 1), (0, 2), (2, 0))
@@ -58,19 +62,19 @@
     return lax.rem(y + YS - o, YS) * 2 + core
 
 
-def y_peer(o):
-    _, col, y, core, _, _ = place()
-    return (lax.rem(y + o, YS) * 2 + core, col)
-
-
 def sibling():
     _, col, y, core, _, _ = place()
     return (y * 2 + 1 - core, col)
 
 
-def x_peer(o):
-    row, _, _, _, x, z = place()
-    return (row, lax.rem(x + o, XS) * ZS + z)
+def cross_peer(o):
+    _, _, y, core, x, z = place()
+    return (y * 2 + 1 - core, lax.rem(x + o, XS) * ZS + z)
+
+
+def plane_peer(oy, ox):
+    _, _, y, core, x, z = place()
+    return (lax.rem(y + oy, YS) * 2 + core, lax.rem(x + ox, XS) * ZS + z)
 
 
 def z_peer(o):
@@ -89,6 +93,14 @@
     )
     copy.start()
     return copy
+
+
+def pack(values):
+    return jnp.concatenate([values[0:6, t * 128 : (t + 1) * 128] for t in range(ACT // 128)], 0)
+
+
+def unpack(tiles):
+    return jnp.concatenate([tiles[6 * t : 6 * t + 6] for t in range(ACT // 128)], 1)
 
 
 def dither(lanes):
@@ -163,9 +175,8 @@
     w0,
     w1,
     part,
-    sum_x,
-    sum_mid,
     sum_z,
+    plane,
     tot,
     in_sem,
     fy_s,
@@ -176,16 +187,15 @@
     ax_r,
     az_s,
     az_r,
-    sx_s,
-    sx_r,
     sz_s,
     sz_r,
-    ty_s,
-    ty_r,
+    sp_s,
+    sp_r,
     tc_s,
     tc_r,
 ):
-    row, col, _, core, _, _ = place()
+    row, col, y_at, core, x_at, _ = place()
+    other = row + 1 - 2 * core
     loads = [
         pltpu.make_async_copy(src, dst, in_sem.at[i])
         for i, (src, dst) in enumerate(((stars_in, stars), (elapsed_in, elapsed), (ids_in, ids)))
@@ -195,8 +205,8 @@
     barrier = pltpu.get_barrier_semaphore()
     peers = (
         [sibling()]
-        + [y_peer(o) for o in range(1, YS)]
-        + [x_peer(o) for o in range(1, XS)]
+        + [plane_peer(oy, ox) for oy, ox in PLANE]
+        + [cross_peer(o) for o in range(1, XS)]
         + [z_peer(o) for o in range(1, ZS)]
     )
     for peer in peers:
@@ -213,41 +223,40 @@
     field[row, 6:7, :] = stars[12:13, :]
     star = ids[...]
     field[row, 7:8, :] = jnp.concatenate([star.astype(F32), jnp.zeros((1, STARS - ACT), F32)], 1)
+    pl.semaphore_wait(barrier, len(peers))
+
+    waits = []
+    own = field.at[row]
+    over_y = {o: send(own, own, fy_s.at[o - 1], fy_r.at[o - 1], plane_peer(o, 0)) for o in Y_ORDER}
+    over_core = [send(own, own, fc_s.at[0], fc_r.at[0], sibling())]
     centre_x = jnp.floor(jnp.sum(x, axis=1, keepdims=True) * (8.0 / STARS) + 0.5) * 0.125
     centre_v = jnp.floor(jnp.sum(v, axis=1, keepdims=True) * (8.0 / STARS) + 0.5) * 0.125
-    pl.semaphore_wait(barrier, len(peers))
-
-    waits = []
-    own = field.at[row]
-    over_y = {o: send(own, own, fy_s.at[o - 1], fy_r.at[o - 1], y_peer(o)) for o in (1, 3, 2)}
-    over_core = [send(own, own, fc_s.at[0], fc_r.at[0], sibling())]
-
+
+    over_core[0].wait_recv()
+    star = jnp.concatenate([star, field[other, 7:8, 0:ACT].astype(jnp.int32)], 1)
     owner = star // STARS
     code = jnp.where(owner % COLS == col, owner // COLS * 16 + star % STARS // 128, -1)
     one_hot = jnp.where(
-        lax.broadcasted_iota(jnp.int32, (128, ACT), 0) == star % 128, 1.0, 0.0
+        lax.broadcasted_iota(jnp.int32, (128, 2 * ACT), 0) == star % 128, 1.0, 0.0
     ).astype(BF16)
     one_hot = jnp.concatenate([one_hot] * 3, 0)
 
-    def pick(r):
+    def pick(r, total):
         block = jnp.concatenate([field[r, :, g * 128 : (g + 1) * 128] for g in range(16)], 0)
         parts = jnp.concatenate(split3(block), 1).astype(BF16)
         hits = jnp.dot(parts, one_hot, preferred_element_type=F32)
-        total = jnp.zeros((8, ACT), F32)
         for g in range(16):
             total = total + jnp.where(code == r * 16 + g, hits[g * 8 : (g + 1) * 8], 0.0)
-        found[...] += total
-
-    found[...] = jnp.zeros_like(found)
-    pick(row)
+        return total
+
+    picks = pick(row, jnp.zeros((8, 2 * ACT), F32))
     for o in (1, 3, 2):
         over_y[o].wait_recv()
         block = field.at[row_from(o)]
         over_core.append(send(block, block, fc_s.at[o], fc_r.at[o], sibling()))
-        pick(row_from(o))
-    for c, o in zip(over_core, (0, 1, 3, 2)):
-        c.wait_recv()
-        pick(row_from(o) + 1 - 2 * core)
+        picks = pick(row_from(o), picks)
+    found[0] = pack(picks[:, 0:ACT])
+    found[1] = pack(picks[:, ACT : 2 * ACT])
     waits += list(over_y.values()) + over_core
 
     lanes = lax.broadcasted_iota(jnp.int32, (1, STARS), 1)
@@ -275,19 +284,28 @@
         spots[r] = jnp.where(lane_of == at, 1.0, 0.0).astype(BF16)
         return 0
 
-    copies = [
-        send(found, act_x.at[o - 1], ax_s.at[o - 1], ax_r.at[o - 1], x_peer(o))
-        for o in range(1, XS)
-    ]
+    copies = []
+    for o in X_ORDER + (0,):
+        copies.append(send(found.at[1], act_x.at[o], ax_s.at[o], ax_r.at[o], cross_peer(o)))
+        if o:
+            n = XS + o - 1
+            copies.append(
+                send(found.at[0], act_x.at[n], ax_s.at[n], ax_r.at[n], plane_peer(0, o))
+            )
+    for c in over_core[1:]:
+        c.wait_recv()
     factor[...] = dither(lax.broadcasted_iota(jnp.int32, (128, 128), 0))
     lax.fori_loop(0, 4, operands, 0)
     for c in copies:
         c.wait_recv()
     waits += copies
-    act_mid[...] = (found[...] + act_x[0]) + (act_x[1] + act_x[2])
+    mine = found[0]
+    for o in range(2 * XS - 1):
+        mine = mine + act_x[o]
+    act_mid[...] = mine
     copies = [
         send(act_mid, act_z.at[o - 1], az_s.at[o - 1], az_r.at[o - 1], z_peer(o))
-        for o in range(1, ZS)
+        for o in Z_ORDER
     ]
     lax.fori_loop(4, ROWS, operands, 0)
     accum[...] = jnp.zeros_like(accum)
@@ -295,9 +313,9 @@
     for c in copies:
         c.wait_recv()
     waits += copies
-    act = act_mid[...]
     for o in range(ZS - 1):
-        act = act + act_z[o]
+        mine = mine + act_z[o]
+    act = unpack(mine)
     xa, va = act[0:3] - centre_x, act[3:6] - centre_v
     act_w[...] = active_rows(xa, va)
 
@@ -340,56 +358,54 @@
         sums(CHUNKS - 1, w1, h)
     o = accum[...]
     o = o[0:8] + o[8:16] + o[16:24]
-    part[0:3, :] = o[0:3] - xa * o[6:7]
-    part[3:6, :] = o[3:6] - va * o[6:7] - xa * o[7:8]
-    part[6:8, :] = jnp.zeros((2, ACT), F32)
+    part[...] = pack(
+        jnp.concatenate([o[0:3] - xa * o[6:7], o[3:6] - va * o[6:7] - xa * o[7:8]], 0)
+    )
 
     copies = [
-        send(part, sum_x.at[o - 1], sx_s.at[o - 1], sx_r.at[o - 1], x_peer(o))
-        for o in range(1, XS)
+        send(part, sum_z.at[o - 1], sz_s.at[o - 1], sz_r.at[o - 1], z_peer(o)) for o in Z_ORDER
     ]
     for c in copies:
         c.wait_recv()
     waits += copies
-    sum_mid[...] = (part[...] + sum_x[0]) + (sum_x[1] + sum_x[2])
-    copies = [
-        send(sum_mid, sum_z.at[o - 1], sz_s.at[o - 1], sz_r.at[o - 1], z_peer(o))
-        for o in range(1, ZS)
-    ]
-    for c in copies:
-        c.wait_recv()
-    waits += copies
-    total = ((sum_mid[...] + sum_z[0]) + (sum_z[1] + sum_z[2])) + (
+    plane[y_at, x_at] = ((part[...] + sum_z[0]) + (sum_z[1] + sum_z[2])) + (
         (sum_z[3] + sum_z[4]) + (sum_z[5] + sum_z[6])
     )
-    tot[row, 0:6, :] = total[0:6]
-    tot[row, 6:7, :] = jnp.zeros((1, ACT), F32)
-    tot[row, 7:8, :] = jnp.ones((1, ACT), F32)
-    own = tot.at[row]
-    over_y = {o: send(own, own, ty_s.at[o - 1], ty_r.at[o - 1], y_peer(o)) for o in (1, 3, 2)}
-    over_core = [send(own, own, tc_s.at[0], tc_r.at[0], sibling())]
+    own = plane.at[y_at, x_at]
+    over_plane = {}
+    for oy, ox in PLANE:
+        n = oy * XS + ox
+        over_plane[oy, ox] = send(own, own, sp_s.at[n], sp_r.at[n], plane_peer(oy, ox))
 
     first = (row * COLS + col) * STARS
 
     def scatter(r):
         local = field[r, 7:8, 0:ACT].astype(jnp.int32) - first
         group = jnp.where((local >= 0) & (local < STARS), local // SPAN, -1)
-        parts = jnp.concatenate(split3(tot[r]), 0)
+        ones = jnp.ones((1, ACT), F32)
+        rows = jnp.concatenate([unpack(tot[r]), 0.0 * ones, ones], 0)
+        parts = jnp.concatenate(split3(rows), 0)
         lhs = jnp.concatenate([jnp.where(group == g, parts, 0.0) for g in range(GROUPS)], 0)
         return lax.dot_general(
             lhs.astype(BF16), spots[r], (((1,), (1,)), ((), ())), preferred_element_type=F32
         )
 
-    placed = scatter(row)
-    for o in (1, 3, 2):
-        over_y[o].wait_recv()
-        block = tot.at[row_from(o)]
-        over_core.append(send(block, block, tc_s.at[o], tc_r.at[o], sibling()))
-        placed = placed + scatter(row_from(o))
-    for c, o in zip(over_core, (0, 1, 3, 2)):
+    placed = jnp.zeros((GROUPS * 24, SPAN), F32)
+    over_core = []
+    for oy in (0, 1, 3, 2):
+        for ox in (1, 3, 2, 0):
+            if (oy, ox) in over_plane:
+                over_plane[oy, ox].wait_recv()
+        y = lax.rem(y_at + YS - oy, YS)
+        r = row_from(oy)
+        tot[r] = (plane[y, 0] + plane[y, 1]) + (plane[y, 2] + plane[y, 3])
+        block = tot.at[r]
+        over_core.append(send(block, block, tc_s.at[oy], tc_r.at[oy], sibling()))
+        placed = placed + scatter(r)
+    for c, oy in zip(over_core, (0, 1, 3, 2)):
         c.wait_recv()
-        placed = placed + scatter(row_from(o) + 1 - 2 * core)
-    waits += list(over_y.values()) + over_core
+        placed = placed + scatter(row_from(oy) + 1 - 2 * core)
+    waits += list(over_plane.values()) + over_core
     new = jnp.concatenate(
         [
             placed[g * 24 : g * 24 + 8]
@@ -415,24 +431,17 @@
 
 def scratch():
     dma = pltpu.SemaphoreType.DMA
-
-    def sums():
-        return [
-            pltpu.VMEM((8, ACT), F32),
-            pltpu.VMEM((XS - 1, 8, ACT), F32),
-            pltpu.VMEM((8, ACT), F32),
-            pltpu.VMEM((ZS - 1, 8, ACT), F32),
-        ]
-
+    packed = (6 * ACT // 128, 128)
     return (
         [
             pltpu.VMEM((13, STARS), F32),
             pltpu.VMEM((1, STARS), F32),
             pltpu.VMEM((1, ACT), jnp.int32),
             pltpu.VMEM((ROWS, 8, STARS), F32),
-        ]
-        + sums()
-        + [
+            pltpu.VMEM((2, *packed), F32),
+            pltpu.VMEM((2 * XS - 1, *packed), F32),
+            pltpu.VMEM(packed, F32),
+            pltpu.VMEM((ZS - 1, *packed), F32),
             pltpu.VMEM((ROWS * STARS, 128), BF16),
             pltpu.VMEM((CHUNKS, 32, 2 * CHUNK), BF16),
             pltpu.VMEM((ROWS, SPAN, ACT), BF16),
@@ -443,12 +452,16 @@
             pltpu.VMEM((CHUNK, 2 * ACT), F32),
             pltpu.VMEM((2 * CHUNK, ACT), BF16),
             pltpu.VMEM((2 * CHUNK, ACT), BF16),
+            pltpu.VMEM(packed, F32),
+            pltpu.VMEM((ZS - 1, *packed), F32),
+            pltpu.VMEM((YS, XS, *packed), F32),
+            pltpu.VMEM((ROWS, *packed), F32),
+            dma((3,)),
         ]
-        + sums()
-        + [pltpu.VMEM((ROWS, 8, ACT), F32), dma((3,))]
         + [dma((n,)) for n in (YS - 1, YS - 1, YS, YS)]
-        + [dma((n,)) for n in (XS - 1, XS - 1, ZS - 1, ZS - 1) * 2]
-        + [dma((n,)) for n in (YS - 1, YS - 1, YS, YS)]
+        + [dma((n,)) for n in (2 * XS - 1, 2 * XS - 1)]
+        + [dma((n,)) for n in (ZS - 1, ZS - 1) * 2]
+        + [dma((n,)) for n in (YS * XS, YS * XS, YS, YS)]
     )
 
 

time: 55.1 us -> 51.6 us (0.936)
  Pallas kernels: 54.4 us -> 50.8 us
    pallas_call x1, Pallas kernels: 54.4 us -> 50.8 us  [local(): pl.pallas_call(kernel, out_shape=pltpu.VMEM((13, STARS), F32), in_specs=[...]
where the time goes in v4:
time: 51.6 us; the launch traced here: 51.5 us
  Pallas kernels  50.8 us (98%)
  local copies, waits for them, and re-layouts  0.66 us (1%)
    pallas_call x1, Pallas kernels, local(): pl.pallas_call(kernel, out_shape=pltpu.VMEM((13, STARS), F32), in_specs=[...  50.8 us

profile of v4, /device:TPU:1, one launch (start us, length us, event | category | flops | bytes accessed | tf_op | source)
XLA Modules:
  0.0 51.5 jit_solution(2405574901693307109)
XLA Ops:
  0.0 50.8 %hermite_step.1 = f32[13,2048]{1,0:T(8,128)S(1)} custom-call(f32[13,2048]{1,0:T(8,128)} %stars_in.1, f32[1,2048]{1,0:T(1,128)} %bitcast.2, s32[1,512]{1,0:T(1,128)} %bitcast.3), custom_call_target="tpu_custom_call" | custom-call | tf_op jit(solution)/shard_map/hermite_step/pallas_call | solution.py:469
  50.8 0.7 %copy.5 = f32[13,2048]{1,0:T(8,128)} copy(f32[13,2048]{1,0:T(8,128)S(1)} %hermite_step.1) | data formatting | bytes 212992

commit v5 on v4

--- a/solution.py
+++ b/solution.py
@@ -28,7 +28,6 @@
 PLANE = [(oy, ox) for oy in (2, 1, 3, 0) for ox in (2, 1, 3, 0) if (oy, ox) != (0, 0)]
 SPAN = 256
 GROUPS = STARS // SPAN
-SPLIT_PAIRS = ((0, 0), (0, 1), (1, 0), (1, 1), (0, 2), (2, 0))
 SOFTEN_HI = float(np.float32(SOFTEN).astype(jnp.bfloat16))
 SOFTEN_LO = float(np.float32(SOFTEN - SOFTEN_HI).astype(jnp.bfloat16))
 VMEM = pl.BlockSpec(memory_space=pltpu.VMEM)
@@ -109,33 +108,37 @@
 
 def field_rows(x, v):
     coarse, fine = split_grid(x)
+    coarse_v, fine_v = split_grid(v)
     one = jnp.ones_like(x[0:1])
     zero = jnp.zeros_like(one)
     big = split3(dot3(coarse, coarse))
     small = split3(dot3(2.0 * coarse + fine, fine))
+    big_d = split3(dot3(coarse, coarse_v))
+    small_d = split3(dot3(coarse, fine_v) + dot3(fine, v))
     hi, mid, lo = split3(fine)
-    radial = split3(jnp.concatenate([v, x, dot3(x, v), one], 0))
+    hi_v, mid_v, lo_v = split3(fine_v)
     return jnp.concatenate(
-        [*big, one, one, one, -2.0 * coarse]
-        + [zero] * 7
+        [*big, one, one, one, -2.0 * coarse, *big_d, coarse_v, zero]
         + [-2.0 * coarse] * 3
         + [hi, mid, lo, -2.0 * hi, -2.0 * hi, -2.0 * mid, -2.0 * mid, *small]
         + [one] * 5
-        + [zero] * 10
-        + [radial[q] for _, q in SPLIT_PAIRS]
-        + [zero] * 16,
+        + [*small_d, hi_v, mid_v, lo_v, coarse_v, coarse_v, coarse_v, hi_v, hi_v, mid_v, mid_v]
+        + [zero] * 41,
         0,
     )
 
 
 def active_rows(x, v):
     coarse, fine = split_grid(x)
+    coarse_v, fine_v = split_grid(v)
     one = jnp.ones_like(x[0:1])
     zero = jnp.zeros_like(one)
     big = split3(dot3(coarse, coarse))
     small = split3(dot3(2.0 * coarse + fine, fine))
+    big_d = split3(dot3(coarse, coarse_v))
+    small_d = split3(dot3(coarse, fine_v) + dot3(fine, v))
     hi, mid, lo = split3(fine)
-    radial = split3(jnp.concatenate([-x, -v, one, dot3(x, v)], 0))
+    hi_v, mid_v, lo_v = split3(0.5 * fine_v)
     for_q = jnp.concatenate(
         [one, one, one, *big, coarse]
         + [zero] * 7
@@ -146,7 +149,14 @@
         0,
     )
     for_d = jnp.concatenate(
-        [zero] * 64 + [radial[p] for p, _ in SPLIT_PAIRS] + [zero] * 16, 0
+        [zero, zero, zero, *big_d, 0.5 * coarse_v, one, one, one, -coarse, zero]
+        + [hi_v, mid_v, lo_v]
+        + [-coarse_v] * 3
+        + [hi_v, mid_v, hi_v, mid_v, zero, zero, zero, *small_d, zero, zero, one, one, one]
+        + [-coarse] * 3
+        + [-hi, -mid, -lo, -hi, -mid, -hi, -mid]
+        + [zero] * 41,
+        0,
     )
     return jnp.concatenate([for_q, for_d], 1).astype(BF16)
 

time: 51.6 us -> 51.6 us (level)
  no operation moved by 1% of the time
where the time goes in v5:
time: 51.6 us; the launch traced here: 51.5 us
  Pallas kernels  50.8 us (98%)
  local copies, waits for them, and re-layouts  0.66 us (1%)
    pallas_call x1, Pallas kernels, local(): pl.pallas_call(kernel, out_shape=pltpu.VMEM((13, STARS), F32), in_specs=[...  50.8 us

profile of v5, /device:TPU:1, one launch (start us, length us, event | category | flops | bytes accessed | tf_op | source)
XLA Modules:
  0.0 51.5 jit_solution(608550492484960596)
XLA Ops:
  0.0 50.8 %hermite_step.1 = f32[13,2048]{1,0:T(8,128)S(1)} custom-call(f32[13,2048]{1,0:T(8,128)} %stars_in.1, f32[1,2048]{1,0:T(1,128)} %bitcast.2, s32[1,512]{1,0:T(1,128)} %bitcast.3), custom_call_target="tpu_custom_call" | custom-call | tf_op jit(solution)/shard_map/hermite_step/pallas_call | solution.py:479
  50.8 0.7 %copy.5 = f32[13,2048]{1,0:T(8,128)} copy(f32[13,2048]{1,0:T(8,128)S(1)} %hermite_step.1) | data formatting | bytes 212992

commit v6 on v5

--- a/solution.py
+++ b/solution.py
@@ -19,13 +19,14 @@
 CHUNK = 256
 PER_SLOT = STARS // CHUNK
 CHUNKS = ROWS * PER_SLOT
-UNROLL = 16
+UNROLL = 32
 HALF = 256
 BLOCK = 64
 Y_ORDER = (2, 1, 3)
 X_ORDER = (2, 1, 3)
 Z_ORDER = (4, 3, 5, 2, 6, 1, 7)
-PLANE = [(oy, ox) for oy in (2, 1, 3, 0) for ox in (2, 1, 3, 0) if (oy, ox) != (0, 0)]
+PLANE = [(2, 2), (2, 1), (2, 3), (1, 2), (3, 2), (1, 1), (1, 3), (3, 1), (3, 3)]
+PLANE += [(2, 0), (0, 2), (1, 0), (3, 0), (0, 1), (0, 3)]
 SPAN = 256
 GROUPS = STARS // SPAN
 SOFTEN_HI = float(np.float32(SOFTEN).astype(jnp.bfloat16))
@@ -214,10 +215,10 @@
         c.start()
     barrier = pltpu.get_barrier_semaphore()
     peers = (
-        [sibling()]
+        [z_peer(o) for o in Z_ORDER]
         + [plane_peer(oy, ox) for oy, ox in PLANE]
-        + [cross_peer(o) for o in range(1, XS)]
-        + [z_peer(o) for o in range(1, ZS)]
+        + [cross_peer(o) for o in X_ORDER]
+        + [sibling()]
     )
     for peer in peers:
         pl.semaphore_signal(barrier, inc=1, device_id=peer, device_id_type=pl.DeviceIdType.MESH)

time: 51.6 us -> 51.2 us (level)
  no operation moved by 1% of the time
where the time goes in v6:
time: 51.2 us; the launch traced here: 51.1 us
  Pallas kernels  50.5 us (99%)
  local copies, waits for them, and re-layouts  0.66 us (1%)
    pallas_call x1, Pallas kernels, local(): pl.pallas_call(kernel, out_shape=pltpu.VMEM((13, STARS), F32), in_specs=[...  50.5 us

profile of v6, /device:TPU:1, one launch (start us, length us, event | category | flops | bytes accessed | tf_op | source)
XLA Modules:
  0.0 51.1 jit_solution(10862126210355050166)
XLA Ops:
  0.0 50.5 %hermite_step.1 = f32[13,2048]{1,0:T(8,128)S(1)} custom-call(f32[13,2048]{1,0:T(8,128)} %stars_in.1, f32[1,2048]{1,0:T(1,128)} %bitcast.2, s32[1,512]{1,0:T(1,128)} %bitcast.3), custom_call_target="tpu_custom_call" | custom-call | tf_op jit(solution)/shard_map/hermite_step/pallas_call | solution.py:480
  50.5 0.7 %copy.5 = f32[13,2048]{1,0:T(8,128)} copy(f32[13,2048]{1,0:T(8,128)S(1)} %hermite_step.1) | data formatting | bytes 212992
